TPU v7x, 32 devices: a whole 2x2x4 slice. The times are simulated.
32 devices in a mesh: gx: 8 (over z, core), gy: 4 (over y, x).
Axes of the slice: x: 2, y: 2, z: 4, core: 2. Of those that a mesh axis runs over, the one named last changes fastest.
Arguments:
- velocity: float32 [3, 256, 256, 128], P(None, 'gx', 'gy'), may hold values from -6 to 6
- stress: float32 [6, 256, 256, 128], P(None, 'gx', 'gy'), may hold values from -9 to 9
- material: float32 [3, 256, 256, 128], P(None, 'gx', 'gy'), may hold values from 0.3 to 1
- src_x: int32 [2, 64], replicated, may hold values from 0 to 255
- src_y: int32 [2, 64], replicated, may hold values from 0 to 255
- src_amp: float32 [2, 64], replicated, may hold values from -30 to 30
- chan_block: int32 [8192, 1], P(('gx', 'gy')), may hold values from 0 to 31; in each aligned block of 256 rows (0 to 255, 256 to 511, ...) at most 16 rows name the same one
- chan_cell: int32 [8192], P(('gx', 'gy')), may hold values from 0 to 262143
- chan_azimuth: float32 [8192], P(('gx', 'gy')), may hold values from -3.140625 to 3.140625
- gauge: int32 [8192], P(('gx', 'gy')), may hold values from 2 to 16
Outputs:
- velocity_out: float32 [3, 256, 256, 128], P(None, 'gx', 'gy')
- stress_out: float32 [6, 256, 256, 128], P(None, 'gx', 'gy')
- strain_rate: float32 [8192], P(('gx', 'gy'))
Inputs may be any that keep to these rules, and one draw needn't show every extreme that they name: `chan_block`: among the 256 channels of one fibre segment (the channels of one device) no grid block is named more than 16 times, and in every draw some grid block is named exactly 16 times by some segment.
All inputs are finite; a program needn't handle non-finite values.
Results may differ from a plain program's by a relative error of at most 0.00012.
Values sent between devices are 32-bit elements; how exact they have to be, the bound alone decides.
A program may use at most 128 MiB of HBM per device.

v0:
```python
import functools

import jax
import jax.numpy as jnp
import ml_dtypes
import numpy as np
from jax import lax
from jax.experimental import pallas as pl
from jax.experimental.pallas import tpu as pltpu
from jax.sharding import PartitionSpec as P

STEPS = 2
COEFFS = (1225.0 / 1024.0, -245.0 / 3072.0, 49.0 / 5120.0, -5.0 / 7168.0)
DT = 0.2
W = 4
PAD = 8
PLANES = 4
MESH = pl.DeviceIdType.MESH


def depth_weights(depth):
    out = np.zeros((2, 2 * depth, 2 * depth), np.float32)
    for which, shift in ((0, 0), (1, -1)):
        table = np.zeros((depth, depth), np.float64)
        for target in range(depth):
            for order in range(1, 5):
                for source, sign in ((target + shift + order, 1.0), (target + shift + 1 - order, -1.0)):
                    if 0 <= source < depth:
                        table[source, target] += sign * COEFFS[order - 1]
        hi = table.astype(np.float32).astype(ml_dtypes.bfloat16).astype(np.float32)
        lo = (table - hi).astype(np.float32)
        out[which, :depth, :depth] = hi
        out[which, :depth, depth:] = lo
        out[which, depth:, :depth] = hi
    return out.astype(ml_dtypes.bfloat16)


def depth_product(values, weights):
    depth = values.shape[1]
    hi = values.astype(jnp.bfloat16)
    lo = (values - hi.astype(jnp.float32)).astype(jnp.bfloat16)
    both = jnp.concatenate([hi, lo], axis=1)
    out = jnp.dot(both, weights, preferred_element_type=jnp.float32)
    return out[:, :depth] + out[:, depth:]


def weighted(load, forward):
    total = None
    shift = 0 if forward else -1
    for order in range(1, 5):
        term = COEFFS[order - 1] * (load(shift + order) - load(shift + 1 - order))
        total = term if total is None else total + term
    return total


def diff_x(ref, f, x, r0, nr, forward):
    return weighted(lambda k: ref[f, x + (W + k), PAD + r0 : PAD + r0 + nr, :], forward)


def diff_y(ref, f, x, r0, nr, forward):
    return weighted(lambda k: ref[f, x + W, PAD + r0 + k : PAD + r0 + k + nr, :], forward)


def own(ref, f, x, r0, nr):
    return ref[f, x + W, PAD + r0 : PAD + r0 + nr, :]


def stress_parts(v, z_of, x, r0, nr, lam, mu):
    exx = diff_x(v, 0, x, r0, nr, False)
    eyy = diff_y(v, 1, x, r0, nr, False)
    ezz = z_of(0)
    common = (DT * lam) * (exx + eyy + ezz)
    dmu = DT * mu
    dmu2 = 2.0 * dmu
    return (
        common + dmu2 * exx,
        dmu * (z_of(1) + diff_x(v, 2, x, r0, nr, True)),
        dmu * (diff_y(v, 0, x, r0, nr, True) + diff_x(v, 1, x, r0, nr, True)),
        dmu * (z_of(2) + diff_y(v, 2, x, r0, nr, True)),
        common + dmu2 * eyy,
        common + dmu2 * ezz,
    )


def main_kernel(
    sizes, cap, stress, velocity, material, weights, force, incoming,
    s1_out, v2_out, picked_out,
    s0, s1, v0, v1, v2, mat, zs, picks, load_sem, send_sem, recv_sem, out_sem,
):
    nx, ny, depth = sizes
    gx, gy = lax.axis_index("gx"), lax.axis_index("gy")
    last_x, last_y = lax.axis_size("gx") - 1, lax.axis_size("gy") - 1
    sides = (
        (gx > 0, "gx", gx - 1),
        (gx < last_x, "gx", gx + 1),
        (gy > 0, "gy", gy - 1),
        (gy < last_y, "gy", gy + 1),
    )
    fields_of = {"s": ((0, 3), (2, 5)), "v": ((0, 3), (0, 3))}
    rows = (slice(PAD, PAD + ny),)[0]
    planes = slice(W, W + nx)

    loads = [
        pltpu.make_async_copy(stress, s0.at[:, planes, rows, :], load_sem.at[0]),
        pltpu.make_async_copy(velocity, v0, load_sem.at[1]),
        pltpu.make_async_copy(material, mat, load_sem.at[2]),
    ]
    for copy in loads:
        copy.start()

    for ref, kind in ((s0, "s"), (s1, "s"), (v1, "v"), (v2, "v")):
        (xa, xb), (ya, yb) = fields_of[kind]

        @pl.when(gx == 0)
        def _():
            ref[xa:xb, 0:W] = jnp.zeros((xb - xa, W, ny + 2 * PAD, depth), jnp.float32)

        @pl.when(gx == last_x)
        def _():
            ref[xa:xb, W + nx :] = jnp.zeros((xb - xa, W, ny + 2 * PAD, depth), jnp.float32)

        @pl.when(gy == 0)
        def _():
            @pl.loop(0, nx)
            def _(x):
                ref[ya:yb, x + W, 0:PAD] = jnp.zeros((yb - ya, PAD, depth), jnp.float32)

        @pl.when(gy == last_y)
        def _():
            @pl.loop(0, nx)
            def _(x):
                ref[ya:yb, x + W, PAD + ny :] = jnp.zeros((yb - ya, PAD, depth), jnp.float32)

    barrier = pltpu.get_barrier_semaphore()
    for exists, axis, other in sides:
        @pl.when(exists)
        def _():
            pl.semaphore_signal(barrier, inc=1, device_id={axis: other}, device_id_type=MESH)
    count = sum(exists.astype(jnp.int32) for exists, _, _ in sides)
    pl.semaphore_wait(barrier, count)

    def transfer(phase, kind, source, target, side, from_input):
        (xa, xb), (ya, yb) = fields_of[kind]
        ox, oy = (0, 0) if from_input else (W, PAD)
        all_x, all_y = slice(ox, ox + nx), slice(oy, oy + ny)
        if side == 0:
            src = source.at[xa:xb, ox : ox + W, all_y, :]
            dst = target.at[xa:xb, W + nx : 2 * W + nx, rows, :]
        elif side == 1:
            src = source.at[xa:xb, ox + nx - W : ox + nx, all_y, :]
            dst = target.at[xa:xb, 0:W, rows, :]
        elif side == 2:
            src = source.at[ya:yb, all_x, oy : oy + W, :]
            dst = target.at[ya:yb, planes, PAD + ny : PAD + ny + W, :]
        else:
            src = source.at[ya:yb, all_x, oy + ny - W : oy + ny, :]
            dst = target.at[ya:yb, planes, PAD - W : PAD, :]
        return pltpu.make_async_remote_copy(
            src_ref=src, dst_ref=dst,
            send_sem=send_sem.at[phase, side], recv_sem=recv_sem.at[phase, side],
            device_id={sides[side][1]: sides[side][2]}, device_id_type=MESH,
        )

    plan = (("s", stress, s0, True), ("v", v1, v1, False), ("s", s1, s1, False), ("v", v2, v2, False))

    def send(phase, which):
        kind, source, target, from_input = plan[phase]
        for side in which:
            @pl.when(sides[side][0])
            def _():
                transfer(phase, kind, source, target, side, from_input).start()

    def arrive(phase):
        kind, source, target, from_input = plan[phase]
        for side in range(4):
            @pl.when(sides[side ^ 1][0])
            def _():
                transfer(phase, kind, source, target, side, from_input).wait_recv()

    def sent(phase):
        kind, source, target, from_input = plan[phase]
        for side in range(4):
            @pl.when(sides[side][0])
            def _():
                transfer(phase, kind, source, target, side, from_input).wait_send()

    def depth_pass(ref, jobs):
        @pl.loop(0, nx // PLANES)
        def _(i):
            x = i * PLANES
            for slot, (f, forward) in enumerate(jobs):
                block = ref[f, pl.ds(x + W, PLANES), PAD : PAD + ny, :].reshape(PLANES * ny, depth)
                out = depth_product(block, weights[0 if forward else 1])
                zs[slot, pl.ds(x, PLANES)] = out.reshape(PLANES, ny, depth)

    def velocity_plane(step, s, x, r0, nr):
        old = (lambda f: v0[f, x, r0 : r0 + nr, :]) if step == 0 else (lambda f: own(v1, f, x, r0, nr))
        new = v1 if step == 0 else v2
        z = lambda k: zs[k, x, r0 : r0 + nr, :]
        db = DT * mat[2, x, r0 : r0 + nr, :]

        def put(f, value):
            updated = old(f) + db * value
            new[f, x + W, PAD + r0 : PAD + r0 + nr, :] = updated
            if step == 1 and f < 2:
                v0[f, x, r0 : r0 + nr, :] = updated

        put(0, diff_x(s, 0, x, r0, nr, True) + diff_y(s, 2, x, r0, nr, False) + z(0))
        put(1, diff_x(s, 2, x, r0, nr, False) + diff_y(s, 4, x, r0, nr, True) + z(1))
        load = pltpu.roll(force[step, r0 : r0 + nr, :], depth - x, 1)
        lane = lax.broadcasted_iota(jnp.int32, (nr, depth), 1)
        rate = diff_x(s, 1, x, r0, nr, False) + diff_y(s, 3, x, r0, nr, False) + z(2)
        put(2, rate + jnp.where(lane == 0, load, 0.0))

    def stress_plane(x, r0, nr):
        lam, mu = mat[0, x, r0 : r0 + nr, :], mat[1, x, r0 : r0 + nr, :]
        z = lambda k: zs[k, x, r0 : r0 + nr, :]
        for f, change in enumerate(stress_parts(v1, z, x, r0, nr, lam, mu)):
            s1[f, x + W, PAD + r0 : PAD + r0 + nr, :] = own(s0, f, x, r0, nr) + change

    def interior(update):
        @pl.loop(W, nx - W)
        def _(x):
            update(x, 8, ny - 16)

    def edges_y(update):
        @pl.loop(0, nx)
        def _(x):
            update(x, 0, 8)
            update(x, ny - 8, 8)

    def edges_x(update):
        @pl.loop(0, 2 * W)
        def _(i):
            update(jnp.where(i < W, i, i + nx - 2 * W), 8, ny - 16)

    def update_of(phase):
        if phase == 1:
            return stress_plane
        return functools.partial(velocity_plane, phase // 2, s0 if phase == 0 else s1)

    v_jobs = ((1, False), (3, False), (5, True))
    s_jobs = ((2, False), (0, True), (1, True))
    send(0, (2, 3, 0, 1))
    loads[0].wait()
    for phase, (ref, jobs) in enumerate(((s0, v_jobs), (v1, s_jobs), (s1, v_jobs))):
        update = update_of(phase)
        depth_pass(ref, jobs)
        if phase == 0:
            loads[1].wait()
            loads[2].wait()
        interior(update)
        arrive(phase)
        edges_y(update)
        send(phase + 1, (2, 3))
        edges_x(update)
        send(phase + 1, (0, 1))
        if phase == 1:
            s1_copy = pltpu.make_async_copy(s1.at[:, planes, rows, :], s1_out, out_sem.at[0])
            s1_copy.start()

    total = incoming.shape[0]
    shift_x, shift_y = (ny * depth).bit_length() - 1, depth.bit_length() - 1
    lane = lax.broadcasted_iota(jnp.int32, (1, depth), 1)

    @pl.loop(0, total // 8)
    def _(i):
        for j in range(8):
            r = i * 8 + j
            cell = incoming[r]
            safe = jnp.maximum(cell, 0)
            x = lax.shift_right_logical(safe, shift_x)
            y = lax.shift_right_logical(safe, shift_y) & (ny - 1)
            z = jnp.where(cell >= 0, safe & (depth - 1), -1)
            for f in range(2):
                row = v0[f, x, pl.ds(y, 1), :]
                picks[f, pl.ds(r, 1), :] = jnp.where(lane == z, row, 0.0)

    devices = total // cap
    ones = jnp.ones((depth, depth), jnp.float32)
    row_id = lax.broadcasted_iota(jnp.int32, (total, depth), 0)
    lane_id = lax.broadcasted_iota(jnp.int32, (total, depth), 1)
    slot = row_id & (cap - 1)
    spread = jnp.zeros((total, depth), jnp.float32)
    for f in range(2):
        wide = jnp.dot(picks[f], ones, precision=lax.Precision.HIGHEST, preferred_element_type=jnp.float32)
        spread = jnp.where(lane_id == slot + f * cap, wide, spread)
    group = lax.broadcasted_iota(jnp.int32, (devices, total), 1)
    first = lax.broadcasted_iota(jnp.int32, (devices, total), 0) * cap
    member = ((group >= first) & (group < first + cap)).astype(jnp.float32)
    picked_out[...] = jnp.dot(
        member, spread, precision=lax.Precision.HIGHEST, preferred_element_type=jnp.float32
    )

    arrive(3)
    v2_copy = pltpu.make_async_copy(v2, v2_out, out_sem.at[1])
    v2_copy.start()
    for phase in range(4):
        sent(phase)
    s1_copy.wait()
    v2_copy.wait()


def last_kernel(v2, s1, mat, weights, v_out, s_out, zs):
    count, ny, depth = s1.shape[1:]
    x0 = pl.program_id(0) * count
    for slot, (f, which) in enumerate(((2, 1), (0, 0), (1, 0))):
        block = v2[f, pl.ds(x0 + W, count), PAD : PAD + ny, :].reshape(count * ny, depth)
        zs[slot] = depth_product(block, weights[which]).reshape(count, ny, depth)

    @pl.loop(0, count)
    def _(p):
        x = x0 + p
        for f in range(3):
            v_out[f, p] = own(v2, f, x, 0, ny)
        for f, change in enumerate(stress_parts(v2, lambda k: zs[k, p], x, 0, ny, mat[0, p], mat[1, p])):
            s_out[f, p] = s1[f, p] + change


def body(
    velocity, stress, material, src_x, src_y, src_amp, chan_block, chan_cell, chan_azimuth, gauge
):
    nx, ny, depth = material.shape[1:]
    devices = lax.axis_size("gx") * lax.axis_size("gy")
    per_device = chan_cell.shape[0]
    cap = max(2, 2 * per_device // devices)
    target = chan_block[:, 0]
    owners = jnp.arange(devices, dtype=jnp.int32)
    member = (target[:, None] == owners[None, :]).astype(jnp.int32)
    before = jnp.cumsum(member, axis=0) - member
    slot_rank = jnp.sum(before * member, axis=1)
    slot_index = target * cap + slot_rank
    slot_match = (
        slot_index[:, None] == jnp.arange(devices * cap, dtype=jnp.int32)[None, :]
    ).astype(jnp.int32)
    filled = jnp.sum(slot_match, axis=0)
    chosen = jnp.sum(slot_match * chan_cell[:, None], axis=0)
    requests = jnp.where(filled > 0, chosen, -1).reshape(devices, cap)
    incoming = lax.all_to_all(requests, ("gx", "gy"), split_axis=0, concat_axis=0, tiled=True)

    anchor_x, anchor_y = lax.axis_index("gx") * nx, lax.axis_index("gy") * ny
    hit_x = (src_x[:, None, :] - anchor_x == jnp.arange(depth, dtype=jnp.int32)[None, :, None]).astype(jnp.float32)
    hit_y = (src_y[:, None, :] - anchor_y == jnp.arange(ny, dtype=jnp.int32)[None, :, None]).astype(jnp.float32)
    force = jnp.einsum("syk,sxk->syx", hit_y, hit_x * src_amp[:, None, :], precision=lax.Precision.HIGHEST)

    weights = jnp.asarray(depth_weights(depth))
    f32 = jnp.float32
    ext = (nx + 2 * W, ny + 2 * PAD, depth)
    total = devices * cap
    any_space = pl.BlockSpec(memory_space=pl.ANY)
    vmem = pl.BlockSpec(memory_space=pltpu.VMEM)
    s1, v2, picked = pl.pallas_call(
        functools.partial(main_kernel, (nx, ny, depth), cap),
        out_shape=(
            jax.ShapeDtypeStruct((6, nx, ny, depth), f32),
            jax.ShapeDtypeStruct((3,) + ext, f32),
            jax.ShapeDtypeStruct((devices, depth), f32),
        ),
        in_specs=[any_space] * 3 + [vmem, vmem, pl.BlockSpec(memory_space=pltpu.SMEM)],
        out_specs=(any_space, any_space, vmem),
        scratch_shapes=[
            pltpu.VMEM((6,) + ext, f32),
            pltpu.VMEM((6,) + ext, f32),
            pltpu.VMEM((3, nx, ny, depth), f32),
            pltpu.VMEM((3,) + ext, f32),
            pltpu.VMEM((3,) + ext, f32),
            pltpu.VMEM((3, nx, ny, depth), f32),
            pltpu.VMEM((3, nx, ny, depth), f32),
            pltpu.VMEM((2, total, depth), f32),
            pltpu.SemaphoreType.DMA((3,)),
            pltpu.SemaphoreType.DMA((4, 4)),
            pltpu.SemaphoreType.DMA((4, 4)),
            pltpu.SemaphoreType.DMA((2,)),
        ],
        compiler_params=pltpu.CompilerParams(
            collective_id=0, has_side_effects=True, vmem_limit_bytes=52 * 2**20
        ),
        cost_estimate=pl.CostEstimate(flops=2 * 10**9, bytes_accessed=24 * 2**20, transcendentals=0),
        name="steps",
    )(stress, velocity, material, weights, force, incoming.reshape(-1))

    chunk = 4
    velocity_out, stress_out = pl.pallas_call(
        last_kernel,
        grid=(nx // chunk,),
        out_shape=(
            jax.ShapeDtypeStruct((3, nx, ny, depth), f32),
            jax.ShapeDtypeStruct((6, nx, ny, depth), f32),
        ),
        in_specs=[
            pl.BlockSpec((3,) + ext, lambda i: (0, 0, 0, 0), pipeline_mode=pl.Buffered(1)),
            pl.BlockSpec((6, chunk, ny, depth), lambda i: (0, i, 0, 0)),
            pl.BlockSpec((2, chunk, ny, depth), lambda i: (0, i, 0, 0)),
            pl.BlockSpec((2, 2 * depth, 2 * depth), lambda i: (0, 0, 0)),
        ],
        out_specs=(
            pl.BlockSpec((3, chunk, ny, depth), lambda i: (0, i, 0, 0)),
            pl.BlockSpec((6, chunk, ny, depth), lambda i: (0, i, 0, 0)),
        ),
        scratch_shapes=[pltpu.VMEM((3, chunk, ny, depth), f32)],
        compiler_params=pltpu.CompilerParams(vmem_limit_bytes=24 * 2**20),
        cost_estimate=pl.CostEstimate(flops=10**9, bytes_accessed=24 * 2**20, transcendentals=0),
        name="last_stress",
    )(v2, s1, material, weights)

    back = jnp.stack([picked[:, :cap], picked[:, cap : 2 * cap]])
    returned = lax.all_to_all(back, ("gx", "gy"), split_axis=1, concat_axis=1, tiled=True)
    flat_back = returned.reshape(2, total)
    values = jnp.sum(slot_match.astype(f32)[None] * flat_back[:, None, :], axis=2)
    along = jnp.cos(chan_azimuth) * values[0] + jnp.sin(chan_azimuth) * values[1]
    route = [(i + 1, i) for i in range(devices - 1)]
    following = lax.ppermute(along, ("gx", "gy"), route)
    joined = jnp.concatenate([along, following])
    offsets = jnp.arange(per_device, dtype=jnp.int32)[:, None] + gauge[:, None]
    ahead_hit = (offsets == jnp.arange(2 * per_device, dtype=jnp.int32)[None, :]).astype(f32)
    ahead = jnp.sum(ahead_hit * joined[None, :], axis=1)
    strain = (ahead - along) / gauge.astype(f32)
    return velocity_out, stress_out, strain


def solution(mesh):
    grid = P(None, "gx", "gy", None)
    line = P(("gx", "gy"))
    return jax.shard_map(
        body,
        mesh=mesh,
        in_specs=(grid, grid, grid, P(), P(), P(), P(("gx", "gy"), None), line, line, line),
        out_specs=(grid, grid, line),
        check_vma=False,
    )
```

profile of v0, /device:TPU:1, one launch (start us, length us, event | category | flops | bytes accessed | tf_op | source)
XLA Modules:
  0.0 96.0 jit_solution(11293592010884381106)
XLA Ops:
  0.6 0.7 fusion.9
  1.3 0.6 reduce-window.6
  1.9 0.2 slice_reduce_fusion
  2.1 0.8 fusion.4
  2.9 0.7 multiply_add_fusion.1
  3.6 0.8 convert_reduce_fusion
  4.4 0.7 select_n.16
  5.1 7.1 %all-to-all-start = ((s32[32,1,16]{2,1,0:T(1,128)}), s32[32,1,16]{2,1,0:T(1,128)S(1)}, u32[]{:S(2)}, u32[]{:S(2)}) async-start(s32[32,1,16]{2,1,0:T(1,128)} %bitcast.5), calls=%async_computation | async-start | bytes 32768 | tf_op jit(solution)/shard_map/all_to_all | solution.py:339
  12.2 0.9 convert_convert_fusion
  13.1 0.7 broadcast_subtract_fusion
  13.8 0.9 fusion.force
  14.8 4.1 %all-to-all-done = s32[32,1,16]{2,1,0:T(1,128)S(1)} async-done(((s32[32,1,16]{2,1,0:T(1,128)}), s32[32,1,16]{2,1,0:T(1,128)S(1)}, u32[]{:S(2)}, u32[]{:S(2)}) %all-to-all-start) | async-done | bytes 2080 | tf_op jit(solution)/shard_map/all_to_all | solution.py:339
  18.8 0.5 broadcast.78
  19.3 0.7 reduce.5
  20.0 0.1 reshape.90.incoming
  20.1 1.0 copy-done.3
  21.1 41.6 %steps.1 = (f32[6,32,64,128]{3,2,1,0:T(8,128)}, f32[3,40,80,128]{3,2,1,0:T(8,128)}, f32[32,128]{1,0:T(8,128)S(1)}) custom-call(f32[6,32,64,128]{3,2,1,0:T(8,128)} %stress.1, f32[3,32,64,128]{3,2,1,0:T(8,128)} %velocity.1, f32[3,32,64,128]{3,2,1,0:T(8,128)} %mat.1, bf16[2,256,256]{2,1,0:T(8,128)(2,1)S(1)} %copy-done.3, f32[2,64,128]{2,1,0:T(8,128)S(1)} %fusion.force, ...), custom_call_target="tpu_custom_call" | custom-call | flops 2000000000 | bytes 25165824 | tf_op jit(solution)/shard_map/steps/pallas_call | solution.py:352
  62.7 0.1 slice_bitcast_fusion.1
  62.8 0.6 copy.21
  63.4 7.2 %all-to-all-start.1 = ((f32[2,32,16]{2,0,1:T(2,128)}), f32[2,32,16]{2,0,1:T(2,128)S(1)}, u32[]{:S(2)}, u32[]{:S(2)}) async-start(f32[2,32,16]{2,0,1:T(2,128)} %copy.21), calls=%async_computation.1 | async-start | bytes 65536 | tf_op jit(solution)/shard_map/all_to_all | solution.py:407
  70.6 0.0 copy-done.5
  70.7 6.7 %all-to-all-done.1 = f32[2,32,16]{2,0,1:T(2,128)S(1)} async-done(((f32[2,32,16]{2,0,1:T(2,128)}), f32[2,32,16]{2,0,1:T(2,128)S(1)}, u32[]{:S(2)}, u32[]{:S(2)}) %all-to-all-start.1) | async-done | bytes 4128 | tf_op jit(solution)/shard_map/all_to_all | solution.py:407
  77.4 0.1 mul.71
  77.5 1.2 %multiply_reduce_fusion = f32[2,256]{1,0:T(2,128)S(1)} fusion(f32[2,512]{1,0:T(2,128)S(1)} %mul.71, f32[256,512]{1,0:T(8,128)} %convert_convert_fusion), kind=kLoop, calls=%fused_computation | loop fusion | flops 523776 | bytes 530432 | tf_op jit(solution)/shard_map/reduce_sum | solution.py:409
  78.7 0.0 copy-done.6
  78.8 2.9 %collective-permute-start = (f32[256]{0:T(256)S(1)}, f32[256]{0:T(256)S(1)}, u32[]{:S(2)}, u32[]{:S(2)}) collective-permute-start(f32[256]{0:T(256)S(1)} %multiply_add_fusion), channel_id=1, source_target_pairs={{1,0},{2,1},{3,2},{4,3},{5,4},{6,5},{7,6},{8,7},{9,8},{10,9},{11,1... | collective-permute-start | bytes 3080 | tf_op jit(solution)/shard_map/ppermute | solution.py:412
  81.7 2.8 %copy-done.1 = f32[6,32,64,128]{3,2,1,0:T(8,128)S(1)} copy-done((f32[6,32,64,128]{3,2,1,0:T(8,128)S(1)}, f32[6,32,64,128]{3,2,1,0:T(8,128)}, u32[]{:S(2)}) %copy-start.1) | copy-done | bytes 6291480
  84.5 2.4 %copy-done.2 = f32[3,40,80,128]{3,2,1,0:T(8,128)S(1)} copy-done((f32[3,40,80,128]{3,2,1,0:T(8,128)S(1)}, f32[3,40,80,128]{3,2,1,0:T(8,128)}, u32[]{:S(2)}) %copy-start.2) | copy-done | bytes 4915224
  86.9 8.3 %last_stress.1 = (f32[3,32,64,128]{3,2,1,0:T(8,128)}, f32[6,32,64,128]{3,2,1,0:T(8,128)}) custom-call(f32[3,40,80,128]{3,2,1,0:T(8,128)S(1)} %copy-done.2, f32[6,32,64,128]{3,2,1,0:T(8,128)S(1)} %copy-done.1, f32[3,32,64,128]{3,2,1,0:T(8,128)S(1)} %copy-done, bf16[2,256,256]{2,1,0:T(8,128)(2,1)S(1)} %copy-done.4), custom_call_target="tpu_custom_call" | custom-call | flops 1000000000 | bytes 25165824 | tf_op jit(solution)/shard_map/last_stress/pallas_call | solution.py:383
  95.2 0.0 collective-permute-done
  95.2 0.2 select_reduce_fusion
  95.4 0.6 convert_divide_fusion
  (18 shorter events, 0.1 us)
Async XLA Ops:
  5.1 13.7 %all-to-all-start = ((s32[32,1,16]{2,1,0:T(1,128)}), s32[32,1,16]{2,1,0:T(1,128)S(1)}, u32[]{:S(2)}, u32[]{:S(2)}) async-start(s32[32,1,16]{2,1,0:T(1,128)} %bitcast.5), calls=%async_computation | async-start | bytes 32768 | tf_op jit(solution)/shard_map/all_to_all | solution.py:339
  20.1 1.0 copy-start.3
  21.1 49.6 %copy-start.5 = (s32[256]{0:T(256)S(1)}, s32[256]{0:T(256)}, u32[]{:S(2)}) copy-start(s32[256]{0:T(256)} %param.20) | copy-start | bytes 3076
  21.1 57.6 %copy-start.6 = (f32[256]{0:T(256)S(1)}, f32[256]{0:T(256)}, u32[]{:S(2)}) copy-start(f32[256]{0:T(256)} %param.19) | copy-start | bytes 3076
  21.1 60.6 %copy-start = (f32[3,32,64,128]{3,2,1,0:T(8,128)S(1)}, f32[3,32,64,128]{3,2,1,0:T(8,128)}, u32[]{:S(2)}) copy-start(f32[3,32,64,128]{3,2,1,0:T(8,128)} %mat.1) | copy-start | bytes 9437188
  21.1 60.6 %copy-start.4 = (bf16[2,256,256]{2,1,0:T(8,128)(2,1)S(1)}, bf16[2,256,256]{2,1,0:T(8,128)(2,1)}, u32[]{:S(2)}) copy-start(bf16[2,256,256]{2,1,0:T(8,128)(2,1)} %constant.31.clone.weights) | copy-start | bytes 786436
  63.4 14.0 %all-to-all-start.1 = ((f32[2,32,16]{2,0,1:T(2,128)}), f32[2,32,16]{2,0,1:T(2,128)S(1)}, u32[]{:S(2)}, u32[]{:S(2)}) async-start(f32[2,32,16]{2,0,1:T(2,128)} %copy.21), calls=%async_computation.1 | async-start | bytes 65536 | tf_op jit(solution)/shard_map/all_to_all | solution.py:407
  78.8 16.5 %collective-permute-start = (f32[256]{0:T(256)S(1)}, f32[256]{0:T(256)S(1)}, u32[]{:S(2)}, u32[]{:S(2)}) collective-permute-start(f32[256]{0:T(256)S(1)} %multiply_add_fusion), channel_id=1, source_target_pairs={{1,0},{2,1},{3,2},{4,3},{5,4},{6,5},{7,6},{8,7},{9,8},{10,9},{11,1... | collective-permute-start | bytes 3080 | tf_op jit(solution)/shard_map/ppermute | solution.py:412
  81.7 2.8 %copy-start.1 = (f32[6,32,64,128]{3,2,1,0:T(8,128)S(1)}, f32[6,32,64,128]{3,2,1,0:T(8,128)}, u32[]{:S(2)}) copy-start(f32[6,32,64,128]{3,2,1,0:T(8,128)} %get-tuple-element.9.s1) | copy-start | bytes 18874372
  84.5 2.4 %copy-start.2 = (f32[3,40,80,128]{3,2,1,0:T(8,128)S(1)}, f32[3,40,80,128]{3,2,1,0:T(8,128)}, u32[]{:S(2)}) copy-start(f32[3,40,80,128]{3,2,1,0:T(8,128)} %get-tuple-element.8.v2) | copy-start | bytes 14745604
where the time goes:
time: 96.5 us; the launch traced here: 96 us
  Pallas kernels  49.9 us (52%)
  starting transfers between devices  17.3 us (18%)
  waiting for transfers between devices  10.8 us (11%)
  local copies, waits for them, and re-layouts  8.42 us (9%)
  other arithmetic  7.93 us (8%)
    pallas_call x1, Pallas kernels, body(): pl.pallas_call(functools.partial(main_kernel, (nx, ny, depth), cap), out_...  41.6 us
    pallas_call x1, Pallas kernels, body(): pl.pallas_call(last_kernel, grid=(nx // chunk,), out_shape=(jax.ShapeDtyp...  8.33 us
    all_to_all x1, starting transfers between devices, body(): lax.all_to_all(back, ('gx', 'gy'), split_axis=1, concat_axis=1, tiled=True)  7.23 us
    all_to_all x1, starting transfers between devices, body(): lax.all_to_all(requests, ('gx', 'gy'), split_axis=0, concat_axis=0, tiled...  7.1 us
    all_to_all x1, waiting for transfers between devices, body(): lax.all_to_all(back, ('gx', 'gy'), split_axis=1, concat_axis=1, tiled=True)  6.72 us
    unnamed x14, local copies, waits for them, and re-layouts  6.14 us
    all_to_all x1, waiting for transfers between devices, body(): lax.all_to_all(requests, ('gx', 'gy'), split_axis=0, concat_axis=0, tiled...  4.07 us
    ppermute x1, starting transfers between devices, body(): following = lax.ppermute(along, ('gx', 'gy'), route)  2.93 us
  transfers between devices with their start and end apart: 3, of which 2 were waited for; matrix products, arithmetic and copies ran while one was open for 3% of the time, Pallas kernels for 9%

commit v1 on v0

--- a/solution.py
+++ b/solution.py
@@ -83,13 +83,17 @@
 
 
 def main_kernel(
-    sizes, cap, stress, velocity, material, weights, force, incoming,
-    s1_out, v2_out, picked_out,
-    s0, s1, v0, v1, v2, mat, zs, picks, load_sem, send_sem, recv_sem, out_sem,
+    sizes, cap, stress, velocity, material, weights, src_x, src_y, src_amp, chan,
+    s1_out, v2_out, strain_out,
+    s0, s1, v0, v1, v2, mat, zs, picks, force, asked, inc, inc_scalar, reply, back, flat, along_ref, follow,
+    load_sem, send_sem, recv_sem, out_sem, ask_send, ask_recv, reply_send, reply_recv, along_sem,
 ):
     nx, ny, depth = sizes
     gx, gy = lax.axis_index("gx"), lax.axis_index("gy")
-    last_x, last_y = lax.axis_size("gx") - 1, lax.axis_size("gy") - 1
+    size_y = lax.axis_size("gy")
+    last_x, last_y = lax.axis_size("gx") - 1, size_y - 1
+    devices = lax.axis_size("gx") * size_y
+    me = gx * size_y + gy
     sides = (
         (gx > 0, "gx", gx - 1),
         (gx < last_x, "gx", gx + 1),
@@ -131,13 +135,34 @@
             def _(x):
                 ref[ya:yb, x + W, PAD + ny :] = jnp.zeros((yb - ya, PAD, depth), jnp.float32)
 
+    def peer(distance):
+        other = lax.rem(me + distance + devices, devices)
+        return {"gx": lax.div(other, size_y), "gy": lax.rem(other, size_y)}
+
     barrier = pltpu.get_barrier_semaphore()
-    for exists, axis, other in sides:
-        @pl.when(exists)
-        def _():
-            pl.semaphore_signal(barrier, inc=1, device_id={axis: other}, device_id_type=MESH)
-    count = sum(exists.astype(jnp.int32) for exists, _, _ in sides)
-    pl.semaphore_wait(barrier, count)
+
+    @pl.loop(1, devices)
+    def _(d):
+        pl.semaphore_signal(barrier, inc=1, device_id=peer(d), device_id_type=MESH)
+
+    pl.semaphore_wait(barrier, devices - 1)
+
+    def ask(d):
+        return pltpu.make_async_remote_copy(
+            src_ref=asked.at[d], dst_ref=inc.at[d], send_sem=ask_send.at[d], recv_sem=ask_recv.at[d],
+            device_id=peer(d), device_id_type=MESH,
+        )
+
+    def answer(d):
+        return pltpu.make_async_remote_copy(
+            src_ref=reply.at[d], dst_ref=back.at[d], send_sem=reply_send.at[d], recv_sem=reply_recv.at[d],
+            device_id=peer(-d), device_id_type=MESH,
+        )
+
+    pass_on = pltpu.make_async_remote_copy(
+        src_ref=along_ref, dst_ref=follow, send_sem=along_sem.at[0], recv_sem=along_sem.at[1],
+        device_id=peer(-1), device_id_type=MESH,
+    )
 
     def transfer(phase, kind, source, target, side, from_input):
         (xa, xb), (ya, yb) = fields_of[kind]
@@ -242,6 +267,41 @@
     v_jobs = ((1, False), (3, False), (5, True))
     s_jobs = ((2, False), (0, True), (1, True))
     send(0, (2, 3, 0, 1))
+
+    segment = chan.shape[1]
+    exact = lax.Precision.HIGHEST
+    f32 = jnp.float32
+    rel = chan[0:1, :].astype(jnp.int32) - me
+    rel = jnp.where(rel < 0, rel + devices, rel)
+    member = (rel == lax.broadcasted_iota(jnp.int32, (devices, segment), 0)).astype(f32)
+    earlier = (
+        lax.broadcasted_iota(jnp.int32, (segment, segment), 0)
+        < lax.broadcasted_iota(jnp.int32, (segment, segment), 1)
+    ).astype(f32)
+    before = jnp.dot(member, earlier, preferred_element_type=f32)
+    rank = jnp.sum(before * member, axis=0, keepdims=True).astype(jnp.int32)
+    slots = lax.broadcasted_iota(jnp.int32, (depth, segment), 0)
+    requests = lax.dot_general(
+        member * (chan[1:2, :] + 1.0), (rank == slots).astype(f32), (((1,), (1,)), ((), ())),
+        precision=exact, preferred_element_type=f32,
+    )
+    requests = (requests + 0.5).astype(jnp.int32) - 1
+    for d in range(devices):
+        asked[d] = requests[d : d + 1, :]
+    inc[0] = requests[0:1, :]
+
+    @pl.loop(1, devices)
+    def _(d):
+        ask(d).start()
+
+    for step in range(STEPS):
+        hit_y = src_y[step : step + 1, :] - gy * ny == lax.broadcasted_iota(jnp.int32, (ny, src_y.shape[1]), 0)
+        hit_x = src_x[step : step + 1, :] - gx * nx == lax.broadcasted_iota(jnp.int32, (depth, src_x.shape[1]), 0)
+        force[step] = lax.dot_general(
+            hit_y.astype(f32), jnp.where(hit_x, src_amp[step : step + 1, :], 0.0), (((1,), (1,)), ((), ())),
+            precision=exact, preferred_element_type=f32,
+        )
+
     loads[0].wait()
     for phase, (ref, jobs) in enumerate(((s0, v_jobs), (v1, s_jobs), (s1, v_jobs))):
         update = update_of(phase)
@@ -259,24 +319,31 @@
             s1_copy = pltpu.make_async_copy(s1.at[:, planes, rows, :], s1_out, out_sem.at[0])
             s1_copy.start()
 
-    total = incoming.shape[0]
+    total = devices * cap
     shift_x, shift_y = (ny * depth).bit_length() - 1, depth.bit_length() - 1
     lane = lax.broadcasted_iota(jnp.int32, (1, depth), 1)
 
-    @pl.loop(0, total // 8)
-    def _(i):
-        for j in range(8):
-            r = i * 8 + j
-            cell = incoming[r]
+    @pl.loop(1, devices)
+    def _(d):
+        ask(d).wait_recv()
+
+    to_scalar = pltpu.make_async_copy(inc, inc_scalar, load_sem.at[3])
+    to_scalar.start()
+    to_scalar.wait()
+
+    @pl.loop(0, devices)
+    def _(d):
+        for j in range(cap):
+            r = d * cap + j
+            cell = inc_scalar[d, 0, j]
             safe = jnp.maximum(cell, 0)
-            x = lax.shift_right_logical(safe, shift_x)
+            x = lax.shift_right_logical(safe, shift_x) & (nx - 1)
             y = lax.shift_right_logical(safe, shift_y) & (ny - 1)
             z = jnp.where(cell >= 0, safe & (depth - 1), -1)
             for f in range(2):
                 row = v0[f, x, pl.ds(y, 1), :]
                 picks[f, pl.ds(r, 1), :] = jnp.where(lane == z, row, 0.0)
 
-    devices = total // cap
     ones = jnp.ones((depth, depth), jnp.float32)
     row_id = lax.broadcasted_iota(jnp.int32, (total, depth), 0)
     lane_id = lax.broadcasted_iota(jnp.int32, (total, depth), 1)
@@ -287,16 +354,64 @@
         spread = jnp.where(lane_id == slot + f * cap, wide, spread)
     group = lax.broadcasted_iota(jnp.int32, (devices, total), 1)
     first = lax.broadcasted_iota(jnp.int32, (devices, total), 0) * cap
-    member = ((group >= first) & (group < first + cap)).astype(jnp.float32)
-    picked_out[...] = jnp.dot(
-        member, spread, precision=lax.Precision.HIGHEST, preferred_element_type=jnp.float32
+    member_rows = ((group >= first) & (group < first + cap)).astype(jnp.float32)
+    picked = jnp.dot(member_rows, spread, precision=exact, preferred_element_type=f32)
+    for d in range(devices):
+        reply[d] = picked[d : d + 1, :]
+    flat[0:1, :] = picked[0:1, :]
+
+    @pl.loop(1, devices)
+    def _(d):
+        answer(d).start()
+
+    @pl.loop(1, devices)
+    def _(d):
+        answer(d).wait_recv()
+
+    for d in range(1, devices):
+        flat[d : d + 1, :] = back[d]
+    columns = lax.dot_general(
+        flat[...], member, (((0,), (0,)), ((), ())), precision=exact, preferred_element_type=f32
     )
+    vel_x = jnp.sum(jnp.where(slots == rank, columns, 0.0), axis=0, keepdims=True)
+    vel_y = jnp.sum(jnp.where(slots == rank + cap, columns, 0.0), axis=0, keepdims=True)
+    along = chan[2:3, :] * vel_x + chan[3:4, :] * vel_y
+    along_ref[...] = along
+
+    @pl.when(me > 0)
+    def _():
+        pass_on.start()
+
+    @pl.when(me == devices - 1)
+    def _():
+        follow[...] = jnp.zeros(follow.shape, f32)
+
+    @pl.when(me < devices - 1)
+    def _():
+        pass_on.wait_recv()
+
+    gauge = chan[4:5, :]
+    joined = jnp.concatenate([along, follow[...]], axis=1)
+    ahead = jnp.zeros((1, segment), f32)
+    for g in range(2, 17):
+        ahead = jnp.where(gauge == g, joined[:, g : g + segment], ahead)
+    strain_out[...] = (ahead - along) / gauge
 
     arrive(3)
     v2_copy = pltpu.make_async_copy(v2, v2_out, out_sem.at[1])
     v2_copy.start()
     for phase in range(4):
         sent(phase)
+
+    @pl.loop(1, devices)
+    def _(d):
+        ask(d).wait_send()
+        answer(d).wait_send()
+
+    @pl.when(me > 0)
+    def _():
+        pass_on.wait_send()
+
     s1_copy.wait()
     v2_copy.wait()
 
@@ -324,39 +439,23 @@
     devices = lax.axis_size("gx") * lax.axis_size("gy")
     per_device = chan_cell.shape[0]
     cap = max(2, 2 * per_device // devices)
-    target = chan_block[:, 0]
-    owners = jnp.arange(devices, dtype=jnp.int32)
-    member = (target[:, None] == owners[None, :]).astype(jnp.int32)
-    before = jnp.cumsum(member, axis=0) - member
-    slot_rank = jnp.sum(before * member, axis=1)
-    slot_index = target * cap + slot_rank
-    slot_match = (
-        slot_index[:, None] == jnp.arange(devices * cap, dtype=jnp.int32)[None, :]
-    ).astype(jnp.int32)
-    filled = jnp.sum(slot_match, axis=0)
-    chosen = jnp.sum(slot_match * chan_cell[:, None], axis=0)
-    requests = jnp.where(filled > 0, chosen, -1).reshape(devices, cap)
-    incoming = lax.all_to_all(requests, ("gx", "gy"), split_axis=0, concat_axis=0, tiled=True)
-
-    anchor_x, anchor_y = lax.axis_index("gx") * nx, lax.axis_index("gy") * ny
-    hit_x = (src_x[:, None, :] - anchor_x == jnp.arange(depth, dtype=jnp.int32)[None, :, None]).astype(jnp.float32)
-    hit_y = (src_y[:, None, :] - anchor_y == jnp.arange(ny, dtype=jnp.int32)[None, :, None]).astype(jnp.float32)
-    force = jnp.einsum("syk,sxk->syx", hit_y, hit_x * src_amp[:, None, :], precision=lax.Precision.HIGHEST)
+    f32 = jnp.float32
+    rows = [chan_block[:, 0].astype(f32), chan_cell.astype(f32), jnp.cos(chan_azimuth), jnp.sin(chan_azimuth)]
+    chan = jnp.stack(rows + [gauge.astype(f32)] * 4)
 
     weights = jnp.asarray(depth_weights(depth))
-    f32 = jnp.float32
     ext = (nx + 2 * W, ny + 2 * PAD, depth)
     total = devices * cap
     any_space = pl.BlockSpec(memory_space=pl.ANY)
     vmem = pl.BlockSpec(memory_space=pltpu.VMEM)
-    s1, v2, picked = pl.pallas_call(
+    s1, v2, strain = pl.pallas_call(
         functools.partial(main_kernel, (nx, ny, depth), cap),
         out_shape=(
             jax.ShapeDtypeStruct((6, nx, ny, depth), f32),
             jax.ShapeDtypeStruct((3,) + ext, f32),
-            jax.ShapeDtypeStruct((devices, depth), f32),
+            jax.ShapeDtypeStruct((1, per_device), f32),
         ),
-        in_specs=[any_space] * 3 + [vmem, vmem, pl.BlockSpec(memory_space=pltpu.SMEM)],
+        in_specs=[any_space] * 3 + [vmem] * 5,
         out_specs=(any_space, any_space, vmem),
         scratch_shapes=[
             pltpu.VMEM((6,) + ext, f32),
@@ -367,9 +466,23 @@
             pltpu.VMEM((3, nx, ny, depth), f32),
             pltpu.VMEM((3, nx, ny, depth), f32),
             pltpu.VMEM((2, total, depth), f32),
-            pltpu.SemaphoreType.DMA((3,)),
+            pltpu.VMEM((STEPS, ny, depth), f32),
+            pltpu.VMEM((devices, 1, depth), jnp.int32),
+            pltpu.VMEM((devices, 1, depth), jnp.int32),
+            pltpu.SMEM((devices, 1, depth), jnp.int32),
+            pltpu.VMEM((devices, 1, depth), f32),
+            pltpu.VMEM((devices, 1, depth), f32),
+            pltpu.VMEM((devices, depth), f32),
+            pltpu.VMEM((1, per_device), f32),
+            pltpu.VMEM((1, per_device), f32),
+            pltpu.SemaphoreType.DMA((4,)),
             pltpu.SemaphoreType.DMA((4, 4)),
             pltpu.SemaphoreType.DMA((4, 4)),
+            pltpu.SemaphoreType.DMA((2,)),
+            pltpu.SemaphoreType.DMA((devices,)),
+            pltpu.SemaphoreType.DMA((devices,)),
+            pltpu.SemaphoreType.DMA((devices,)),
+            pltpu.SemaphoreType.DMA((devices,)),
             pltpu.SemaphoreType.DMA((2,)),
         ],
         compiler_params=pltpu.CompilerParams(
@@ -377,7 +490,7 @@
         ),
         cost_estimate=pl.CostEstimate(flops=2 * 10**9, bytes_accessed=24 * 2**20, transcendentals=0),
         name="steps",
-    )(stress, velocity, material, weights, force, incoming.reshape(-1))
+    )(stress, velocity, material, weights, src_x, src_y, src_amp, chan)
 
     chunk = 4
     velocity_out, stress_out = pl.pallas_call(
@@ -398,24 +511,12 @@
             pl.BlockSpec((6, chunk, ny, depth), lambda i: (0, i, 0, 0)),
         ),
         scratch_shapes=[pltpu.VMEM((3, chunk, ny, depth), f32)],
-        compiler_params=pltpu.CompilerParams(vmem_limit_bytes=24 * 2**20),
+        compiler_params=pltpu.CompilerParams(vmem_limit_bytes=56 * 2**20),
         cost_estimate=pl.CostEstimate(flops=10**9, bytes_accessed=24 * 2**20, transcendentals=0),
         name="last_stress",
     )(v2, s1, material, weights)
 
-    back = jnp.stack([picked[:, :cap], picked[:, cap : 2 * cap]])
-    returned = lax.all_to_all(back, ("gx", "gy"), split_axis=1, concat_axis=1, tiled=True)
-    flat_back = returned.reshape(2, total)
-    values = jnp.sum(slot_match.astype(f32)[None] * flat_back[:, None, :], axis=2)
-    along = jnp.cos(chan_azimuth) * values[0] + jnp.sin(chan_azimuth) * values[1]
-    route = [(i + 1, i) for i in range(devices - 1)]
-    following = lax.ppermute(along, ("gx", "gy"), route)
-    joined = jnp.concatenate([along, following])
-    offsets = jnp.arange(per_device, dtype=jnp.int32)[:, None] + gauge[:, None]
-    ahead_hit = (offsets == jnp.arange(2 * per_device, dtype=jnp.int32)[None, :]).astype(f32)
-    ahead = jnp.sum(ahead_hit * joined[None, :], axis=1)
-    strain = (ahead - along) / gauge.astype(f32)
-    return velocity_out, stress_out, strain
+    return velocity_out, stress_out, strain.reshape(-1)
 
 
 def solution(mesh):

time: 96.5 us -> 76.9 us (0.80)
  the two profiles are of different devices: /device:TPU:1 before, /device:TPU:0 now
where the time goes in v1:
time: 76.9 us; the launch traced here: 76.5 us
  Pallas kernels  69.5 us (90%)
  local copies, waits for them, and re-layouts  4.29 us (6%)
  other arithmetic  2.04 us (3%)
    pallas_call x1, Pallas kernels, body(): pl.pallas_call(functools.partial(main_kernel, (nx, ny, depth), cap), out_...  56.5 us
    pallas_call x1, Pallas kernels, body(): pl.pallas_call(last_kernel, grid=(nx // chunk,), out_shape=(jax.ShapeDtyp...  13 us
    unnamed x9, local copies, waits for them, and re-layouts  3.54 us

profile of v1, /device:TPU:0, one launch (start us, length us, event | category | flops | bytes accessed | tf_op | source)
XLA Modules:
  0.0 76.5 jit_solution(16034336430552130577)
XLA Ops:
  0.6 0.7 convert_bitcast_fusion
  1.3 0.7 convert_element_type.21
  2.0 0.7 convert_element_type.22
  2.7 0.7 fusion
  3.4 0.0 copy-start
  3.4 0.9 %copy-done = bf16[2,256,256]{2,1,0:T(8,128)(2,1)S(1)} copy-done((bf16[2,256,256]{2,1,0:T(8,128)(2,1)S(1)}, bf16[2,256,256]{2,1,0:T(8,128)(2,1)}, u32[]{:S(2)}) %copy-start) | copy-done | bytes 262168
  4.4 0.0 copy-start.1
  4.4 0.7 copy-done.1
  5.1 0.0 copy-start.2
  5.1 0.7 copy-done.2
  5.7 0.0 copy-start.3
  5.7 0.7 copy-done.3
  6.4 56.5 %steps.1 = (f32[6,32,64,128]{3,2,1,0:T(8,128)}, f32[3,40,80,128]{3,2,1,0:T(8,128)}, f32[1,256]{1,0:T(1,128)S(1)}) custom-call(f32[6,32,64,128]{3,2,1,0:T(8,128)} %stress.1, f32[3,32,64,128]{3,2,1,0:T(8,128)} %velocity.1, f32[3,32,64,128]{3,2,1,0:T(8,128)} %mat.1, bf16[2,256,256]{2,1,0:T(8,128)(2,1)S(1)} %copy-done, s32[2,64]{1,0:T(2,128)S(1)} %copy-done.1, ...), custom_call_target="tpu_custom_call" | custom-call | flops 2000000000 | bytes 25165824 | tf_op jit(solution)/shard_map/steps/pallas_call | solution.py:451
  62.9 13.0 %last_stress.1 = (f32[3,32,64,128]{3,2,1,0:T(8,128)}, f32[6,32,64,128]{3,2,1,0:T(8,128)}) custom-call(f32[3,40,80,128]{3,2,1,0:T(8,128)} %get-tuple-element.8.v2, f32[6,32,64,128]{3,2,1,0:T(8,128)} %get-tuple-element.9.s1, f32[3,32,64,128]{3,2,1,0:T(8,128)} %mat.1, bf16[2,256,256]{2,1,0:T(8,128)(2,1)} %constant.2.clone.weights), custom_call_target="tpu_custom_call" | custom-call | flops 1000000000 | bytes 25165824 | tf_op jit(solution)/shard_map/last_stress/pallas_call | solution.py:496
  75.9 0.6 copy.15
  (1 shorter events, 0.0 us)
Async XLA Ops:
  3.4 1.0 %copy-start = (bf16[2,256,256]{2,1,0:T(8,128)(2,1)S(1)}, bf16[2,256,256]{2,1,0:T(8,128)(2,1)}, u32[]{:S(2)}) copy-start(bf16[2,256,256]{2,1,0:T(8,128)(2,1)} %constant.2.clone.weights) | copy-start | bytes 786436
  4.4 0.7 copy-start.1
  5.1 0.7 copy-start.2
  5.7 0.7 copy-start.3

commit v2 on v1

--- a/solution.py
+++ b/solution.py
@@ -14,6 +14,7 @@
 DT = 0.2
 W = 4
 PAD = 8
+PARTS = 4
 PLANES = 4
 MESH = pl.DeviceIdType.MESH
 
@@ -83,10 +84,12 @@
 
 
 def main_kernel(
-    sizes, cap, stress, velocity, material, weights, src_x, src_y, src_amp, chan,
-    s1_out, v2_out, strain_out,
+    sizes, cap, stress, velocity, material, weights_in, src_x_in, src_y_in, src_amp_in,
+    block_in, cell_in, azimuth_in, gauge_in,
+    v_out, s_out, strain_out,
     s0, s1, v0, v1, v2, mat, zs, picks, force, asked, inc, inc_scalar, reply, back, flat, along_ref, follow,
-    load_sem, send_sem, recv_sem, out_sem, ask_send, ask_recv, reply_send, reply_recv, along_sem,
+    weights, src_x, src_y, src_amp, block, cells, azimuth, gauge,
+    load_sem, send_sem, recv_sem, y_send, y_recv, out_sem, ask_send, ask_recv, reply_send, reply_recv, along_sem,
 ):
     nx, ny, depth = sizes
     gx, gy = lax.axis_index("gx"), lax.axis_index("gy")
@@ -101,6 +104,8 @@
         (gy < last_y, "gy", gy + 1),
     )
     fields_of = {"s": ((0, 3), (2, 5)), "v": ((0, 3), (0, 3))}
+    groups_of = {"s": ((2, 4, False), (4, 5, True)), "v": ((0, 1, True), (1, 2, False), (2, 3, True))}
+    part = nx // PARTS
     rows = (slice(PAD, PAD + ny),)[0]
     planes = slice(W, W + nx)
 
@@ -109,7 +114,13 @@
         pltpu.make_async_copy(velocity, v0, load_sem.at[1]),
         pltpu.make_async_copy(material, mat, load_sem.at[2]),
     ]
-    for copy in loads:
+    small = (
+        (weights_in, weights), (src_x_in, src_x), (src_y_in, src_y), (src_amp_in, src_amp),
+        (block_in, block), (cell_in, cells), (azimuth_in, azimuth), (gauge_in, gauge),
+    )
+    for number, (source, target) in enumerate(small):
+        loads.append(pltpu.make_async_copy(source, target, load_sem.at[4 + number]))
+    for copy in loads[3:] + loads[:3]:
         copy.start()
 
     for ref, kind in ((s0, "s"), (s1, "s"), (v1, "v"), (v2, "v")):
@@ -164,50 +175,61 @@
         device_id=peer(-1), device_id_type=MESH,
     )
 
-    def transfer(phase, kind, source, target, side, from_input):
-        (xa, xb), (ya, yb) = fields_of[kind]
+    plan = (("s", stress, s0, True), ("v", v1, v1, False), ("s", s1, s1, False), ("v", v2, v2, False))
+
+    def transfer_x(phase, side):
+        kind, source, target, from_input = plan[phase]
+        xa, xb = fields_of[kind][0]
         ox, oy = (0, 0) if from_input else (W, PAD)
-        all_x, all_y = slice(ox, ox + nx), slice(oy, oy + ny)
-        if side == 0:
-            src = source.at[xa:xb, ox : ox + W, all_y, :]
-            dst = target.at[xa:xb, W + nx : 2 * W + nx, rows, :]
-        elif side == 1:
-            src = source.at[xa:xb, ox + nx - W : ox + nx, all_y, :]
-            dst = target.at[xa:xb, 0:W, rows, :]
-        elif side == 2:
-            src = source.at[ya:yb, all_x, oy : oy + W, :]
-            dst = target.at[ya:yb, planes, PAD + ny : PAD + ny + W, :]
-        else:
-            src = source.at[ya:yb, all_x, oy + ny - W : oy + ny, :]
-            dst = target.at[ya:yb, planes, PAD - W : PAD, :]
+        start, landing = (ox, W + nx) if side == 0 else (ox + nx - W, 0)
         return pltpu.make_async_remote_copy(
-            src_ref=src, dst_ref=dst,
+            src_ref=source.at[xa:xb, start : start + W, oy : oy + ny, :],
+            dst_ref=target.at[xa:xb, landing : landing + W, rows, :],
             send_sem=send_sem.at[phase, side], recv_sem=recv_sem.at[phase, side],
-            device_id={sides[side][1]: sides[side][2]}, device_id_type=MESH,
+            device_id={"gx": sides[side][2]}, device_id_type=MESH,
         )
 
-    plan = (("s", stress, s0, True), ("v", v1, v1, False), ("s", s1, s1, False), ("v", v2, v2, False))
-
-    def send(phase, which):
+    def transfers_y(phase, side, piece):
         kind, source, target, from_input = plan[phase]
+        ox, oy = (0, 0) if from_input else (W, PAD)
+        first = piece * part
+        out = []
+        for number, (ya, yb, forward) in enumerate(groups_of[kind]):
+            width = W if forward == (side == 2) else W - 1
+            start, landing = (oy, PAD + ny) if side == 2 else (oy + ny - width, PAD - width)
+            out.append(pltpu.make_async_remote_copy(
+                src_ref=source.at[ya:yb, ox + first : ox + first + part, start : start + width, :],
+                dst_ref=target.at[ya:yb, W + first : W + first + part, landing : landing + width, :],
+                send_sem=y_send.at[phase, side - 2, piece, number],
+                recv_sem=y_recv.at[phase, side - 2, piece, number],
+                device_id={"gy": sides[side][2]}, device_id_type=MESH,
+            ))
+        return out
+
+    def copies(phase, side, piece):
+        return [transfer_x(phase, side)] if side < 2 else transfers_y(phase, side, piece)
+
+    def send(phase, which, piece=0):
         for side in which:
             @pl.when(sides[side][0])
             def _():
-                transfer(phase, kind, source, target, side, from_input).start()
-
-    def arrive(phase):
-        kind, source, target, from_input = plan[phase]
-        for side in range(4):
+                for copy in copies(phase, side, piece):
+                    copy.start()
+
+    def arrive(phase, which, piece=0):
+        for side in which:
             @pl.when(sides[side ^ 1][0])
             def _():
-                transfer(phase, kind, source, target, side, from_input).wait_recv()
+                for copy in copies(phase, side, piece):
+                    copy.wait_recv()
 
     def sent(phase):
-        kind, source, target, from_input = plan[phase]
         for side in range(4):
             @pl.when(sides[side][0])
             def _():
-                transfer(phase, kind, source, target, side, from_input).wait_send()
+                for piece in range(PARTS if side > 1 else 1):
+                    for copy in copies(phase, side, piece):
+                        copy.wait_send()
 
     def depth_pass(ref, jobs):
         @pl.loop(0, nx // PLANES)
@@ -237,19 +259,19 @@
         rate = diff_x(s, 1, x, r0, nr, False) + diff_y(s, 3, x, r0, nr, False) + z(2)
         put(2, rate + jnp.where(lane == 0, load, 0.0))
 
-    def stress_plane(x, r0, nr):
+    def stress_plane(v, s, new, x, r0, nr):
         lam, mu = mat[0, x, r0 : r0 + nr, :], mat[1, x, r0 : r0 + nr, :]
         z = lambda k: zs[k, x, r0 : r0 + nr, :]
-        for f, change in enumerate(stress_parts(v1, z, x, r0, nr, lam, mu)):
-            s1[f, x + W, PAD + r0 : PAD + r0 + nr, :] = own(s0, f, x, r0, nr) + change
+        for f, change in enumerate(stress_parts(v, z, x, r0, nr, lam, mu)):
+            new[f, x + W, PAD + r0 : PAD + r0 + nr, :] = own(s, f, x, r0, nr) + change
 
     def interior(update):
         @pl.loop(W, nx - W)
         def _(x):
             update(x, 8, ny - 16)
 
-    def edges_y(update):
-        @pl.loop(0, nx)
+    def edges_y(update, piece):
+        @pl.loop(piece * part, (piece + 1) * part)
         def _(x):
             update(x, 0, 8)
             update(x, ny - 8, 8)
@@ -259,19 +281,47 @@
         def _(i):
             update(jnp.where(i < W, i, i + nx - 2 * W), 8, ny - 16)
 
-    def update_of(phase):
-        if phase == 1:
-            return stress_plane
-        return functools.partial(velocity_plane, phase // 2, s0 if phase == 0 else s1)
+    updates = (
+        functools.partial(velocity_plane, 0, s0),
+        functools.partial(stress_plane, v1, s0, s1),
+        functools.partial(velocity_plane, 1, s1),
+        functools.partial(stress_plane, v2, s1, s0),
+    )
+
+    def all_edges(phase, done=lambda pieces: None):
+        update = updates[phase]
+
+        def piece_of(piece):
+            arrive(phase, (2, 3), piece)
+            edges_y(update, piece)
+            if phase < 3:
+                send(phase + 1, (2, 3), piece)
+
+        arrive(phase, (0, 1))
+        piece_of(0)
+        piece_of(PARTS - 1)
+        edges_x(update)
+        if phase < 3:
+            send(phase + 1, (0, 1))
+        done((0, PARTS - 1))
+        for piece in range(1, PARTS - 1):
+            piece_of(piece)
+            done((piece,))
 
     v_jobs = ((1, False), (3, False), (5, True))
     s_jobs = ((2, False), (0, True), (1, True))
-    send(0, (2, 3, 0, 1))
-
-    segment = chan.shape[1]
+    for piece in (0, PARTS - 1):
+        send(0, (2, 3), piece)
+    send(0, (0, 1))
+    for piece in range(1, PARTS - 1):
+        send(0, (2, 3), piece)
+    for copy in loads[3:]:
+        copy.wait()
+
+    segment = block.shape[1]
     exact = lax.Precision.HIGHEST
     f32 = jnp.float32
-    rel = chan[0:1, :].astype(jnp.int32) - me
+    rel = block[...] - me
     rel = jnp.where(rel < 0, rel + devices, rel)
     member = (rel == lax.broadcasted_iota(jnp.int32, (devices, segment), 0)).astype(f32)
     earlier = (
@@ -282,7 +332,7 @@
     rank = jnp.sum(before * member, axis=0, keepdims=True).astype(jnp.int32)
     slots = lax.broadcasted_iota(jnp.int32, (depth, segment), 0)
     requests = lax.dot_general(
-        member * (chan[1:2, :] + 1.0), (rank == slots).astype(f32), (((1,), (1,)), ((), ())),
+        member * (cells[...] + 1).astype(f32), (rank == slots).astype(f32), (((1,), (1,)), ((), ())),
         precision=exact, preferred_element_type=f32,
     )
     requests = (requests + 0.5).astype(jnp.int32) - 1
@@ -304,20 +354,14 @@
 
     loads[0].wait()
     for phase, (ref, jobs) in enumerate(((s0, v_jobs), (v1, s_jobs), (s1, v_jobs))):
-        update = update_of(phase)
         depth_pass(ref, jobs)
         if phase == 0:
             loads[1].wait()
             loads[2].wait()
-        interior(update)
-        arrive(phase)
-        edges_y(update)
-        send(phase + 1, (2, 3))
-        edges_x(update)
-        send(phase + 1, (0, 1))
-        if phase == 1:
-            s1_copy = pltpu.make_async_copy(s1.at[:, planes, rows, :], s1_out, out_sem.at[0])
-            s1_copy.start()
+        interior(updates[phase])
+        all_edges(phase)
+    v_copy = pltpu.make_async_copy(v2.at[:, planes, rows, :], v_out, out_sem.at[PARTS])
+    v_copy.start()
 
     total = devices * cap
     shift_x, shift_y = (ny * depth).bit_length() - 1, depth.bit_length() - 1
@@ -364,6 +408,9 @@
     def _(d):
         answer(d).start()
 
+    depth_pass(v2, s_jobs)
+    interior(updates[3])
+
     @pl.loop(1, devices)
     def _(d):
         answer(d).wait_recv()
@@ -375,7 +422,7 @@
     )
     vel_x = jnp.sum(jnp.where(slots == rank, columns, 0.0), axis=0, keepdims=True)
     vel_y = jnp.sum(jnp.where(slots == rank + cap, columns, 0.0), axis=0, keepdims=True)
-    along = chan[2:3, :] * vel_x + chan[3:4, :] * vel_y
+    along = jnp.cos(azimuth[...]) * vel_x + jnp.sin(azimuth[...]) * vel_y
     along_ref[...] = along
 
     @pl.when(me > 0)
@@ -386,20 +433,30 @@
     def _():
         follow[...] = jnp.zeros(follow.shape, f32)
 
+    s_copies = [
+        pltpu.make_async_copy(
+            s0.at[:, W + piece * part : W + (piece + 1) * part, rows, :],
+            s_out.at[:, piece * part : (piece + 1) * part], out_sem.at[piece],
+        )
+        for piece in range(PARTS)
+    ]
+
+    def write(pieces):
+        for piece in pieces:
+            s_copies[piece].start()
+
+    all_edges(3, write)
+
     @pl.when(me < devices - 1)
     def _():
         pass_on.wait_recv()
 
-    gauge = chan[4:5, :]
     joined = jnp.concatenate([along, follow[...]], axis=1)
     ahead = jnp.zeros((1, segment), f32)
     for g in range(2, 17):
-        ahead = jnp.where(gauge == g, joined[:, g : g + segment], ahead)
-    strain_out[...] = (ahead - along) / gauge
-
-    arrive(3)
-    v2_copy = pltpu.make_async_copy(v2, v2_out, out_sem.at[1])
-    v2_copy.start()
+        ahead = jnp.where(gauge[...] == g, joined[:, g : g + segment], ahead)
+    strain_out[...] = (ahead - along) / gauge[...].astype(f32)
+
     for phase in range(4):
         sent(phase)
 
@@ -412,24 +469,9 @@
     def _():
         pass_on.wait_send()
 
-    s1_copy.wait()
-    v2_copy.wait()
-
-
-def last_kernel(v2, s1, mat, weights, v_out, s_out, zs):
-    count, ny, depth = s1.shape[1:]
-    x0 = pl.program_id(0) * count
-    for slot, (f, which) in enumerate(((2, 1), (0, 0), (1, 0))):
-        block = v2[f, pl.ds(x0 + W, count), PAD : PAD + ny, :].reshape(count * ny, depth)
-        zs[slot] = depth_product(block, weights[which]).reshape(count, ny, depth)
-
-    @pl.loop(0, count)
-    def _(p):
-        x = x0 + p
-        for f in range(3):
-            v_out[f, p] = own(v2, f, x, 0, ny)
-        for f, change in enumerate(stress_parts(v2, lambda k: zs[k, p], x, 0, ny, mat[0, p], mat[1, p])):
-            s_out[f, p] = s1[f, p] + change
+    v_copy.wait()
+    for copy in s_copies:
+        copy.wait()
 
 
 def body(
@@ -440,22 +482,19 @@
     per_device = chan_cell.shape[0]
     cap = max(2, 2 * per_device // devices)
     f32 = jnp.float32
-    rows = [chan_block[:, 0].astype(f32), chan_cell.astype(f32), jnp.cos(chan_azimuth), jnp.sin(chan_azimuth)]
-    chan = jnp.stack(rows + [gauge.astype(f32)] * 4)
-
     weights = jnp.asarray(depth_weights(depth))
     ext = (nx + 2 * W, ny + 2 * PAD, depth)
     total = devices * cap
     any_space = pl.BlockSpec(memory_space=pl.ANY)
     vmem = pl.BlockSpec(memory_space=pltpu.VMEM)
-    s1, v2, strain = pl.pallas_call(
+    velocity_out, stress_out, strain = pl.pallas_call(
         functools.partial(main_kernel, (nx, ny, depth), cap),
         out_shape=(
+            jax.ShapeDtypeStruct((3, nx, ny, depth), f32),
             jax.ShapeDtypeStruct((6, nx, ny, depth), f32),
-            jax.ShapeDtypeStruct((3,) + ext, f32),
             jax.ShapeDtypeStruct((1, per_device), f32),
         ),
-        in_specs=[any_space] * 3 + [vmem] * 5,
+        in_specs=[any_space] * 11,
         out_specs=(any_space, any_space, vmem),
         scratch_shapes=[
             pltpu.VMEM((6,) + ext, f32),
@@ -475,10 +514,20 @@
             pltpu.VMEM((devices, depth), f32),
             pltpu.VMEM((1, per_device), f32),
             pltpu.VMEM((1, per_device), f32),
-            pltpu.SemaphoreType.DMA((4,)),
-            pltpu.SemaphoreType.DMA((4, 4)),
-            pltpu.SemaphoreType.DMA((4, 4)),
-            pltpu.SemaphoreType.DMA((2,)),
+            pltpu.VMEM(weights.shape, weights.dtype),
+            pltpu.VMEM(src_x.shape, jnp.int32),
+            pltpu.VMEM(src_y.shape, jnp.int32),
+            pltpu.VMEM(src_amp.shape, f32),
+            pltpu.VMEM((1, per_device), jnp.int32),
+            pltpu.VMEM((1, per_device), jnp.int32),
+            pltpu.VMEM((1, per_device), f32),
+            pltpu.VMEM((1, per_device), jnp.int32),
+            pltpu.SemaphoreType.DMA((12,)),
+            pltpu.SemaphoreType.DMA((4, 2)),
+            pltpu.SemaphoreType.DMA((4, 2)),
+            pltpu.SemaphoreType.DMA((4, 2, PARTS, 3)),
+            pltpu.SemaphoreType.DMA((4, 2, PARTS, 3)),
+            pltpu.SemaphoreType.DMA((PARTS + 1,)),
             pltpu.SemaphoreType.DMA((devices,)),
             pltpu.SemaphoreType.DMA((devices,)),
             pltpu.SemaphoreType.DMA((devices,)),
@@ -486,36 +535,13 @@
             pltpu.SemaphoreType.DMA((2,)),
         ],
         compiler_params=pltpu.CompilerParams(
-            collective_id=0, has_side_effects=True, vmem_limit_bytes=52 * 2**20
+            collective_id=0, has_side_effects=True, vmem_limit_bytes=60 * 2**20
         ),
         cost_estimate=pl.CostEstimate(flops=2 * 10**9, bytes_accessed=24 * 2**20, transcendentals=0),
         name="steps",
-    )(stress, velocity, material, weights, src_x, src_y, src_amp, chan)
-
-    chunk = 4
-    velocity_out, stress_out = pl.pallas_call(
-        last_kernel,
-        grid=(nx // chunk,),
-        out_shape=(
-            jax.ShapeDtypeStruct((3, nx, ny, depth), f32),
-            jax.ShapeDtypeStruct((6, nx, ny, depth), f32),
-        ),
-        in_specs=[
-            pl.BlockSpec((3,) + ext, lambda i: (0, 0, 0, 0), pipeline_mode=pl.Buffered(1)),
-            pl.BlockSpec((6, chunk, ny, depth), lambda i: (0, i, 0, 0)),
-            pl.BlockSpec((2, chunk, ny, depth), lambda i: (0, i, 0, 0)),
-            pl.BlockSpec((2, 2 * depth, 2 * depth), lambda i: (0, 0, 0)),
-        ],
-        out_specs=(
-            pl.BlockSpec((3, chunk, ny, depth), lambda i: (0, i, 0, 0)),
-            pl.BlockSpec((6, chunk, ny, depth), lambda i: (0, i, 0, 0)),
-        ),
-        scratch_shapes=[pltpu.VMEM((3, chunk, ny, depth), f32)],
-        compiler_params=pltpu.CompilerParams(vmem_limit_bytes=56 * 2**20),
-        cost_estimate=pl.CostEstimate(flops=10**9, bytes_accessed=24 * 2**20, transcendentals=0),
-        name="last_stress",
-    )(v2, s1, material, weights)
-
+    )(stress, velocity, material, weights, src_x, src_y, src_amp, *(
+        line.reshape(1, per_device) for line in (chan_block, chan_cell, chan_azimuth, gauge)
+    ))
     return velocity_out, stress_out, strain.reshape(-1)
 
 

time: 76.9 us -> 58.7 us (0.76)
  the two profiles are of different devices: /device:TPU:0 before, /device:TPU:1 now
where the time goes in v2:
time: 58.7 us; the launch traced here: 58.5 us
  Pallas kernels  50.2 us (86%)
  local copies, waits for them, and re-layouts  7.68 us (13%)
  between operations  0.65 us (1%)
    pallas_call x1, Pallas kernels, body(): pl.pallas_call(functools.partial(main_kernel, (nx, ny, depth), cap), out_...  50.2 us
    unnamed x7, local copies, waits for them, and re-layouts  7.68 us

profile of v2, /device:TPU:1, one launch (start us, length us, event | category | flops | bytes accessed | tf_op | source)
XLA Modules:
  0.0 58.5 jit_solution(11742907023098336573)
XLA Ops:
  0.6 50.2 %steps.1 = (f32[3,32,64,128]{3,2,1,0:T(8,128)}, f32[6,32,64,128]{3,2,1,0:T(8,128)}, f32[1,256]{1,0:T(1,128)}) custom-call(f32[6,32,64,128]{3,2,1,0:T(8,128)} %stress.1, f32[3,32,64,128]{3,2,1,0:T(8,128)} %velocity.1, f32[3,32,64,128]{3,2,1,0:T(8,128)} %material.1, bf16[2,256,256]{2,1,0:T(8,128)(2,1)} %constant.2.clone.weights_in, s32[2,64]{1,0:T(2,128)} %src_x_in.1, ...), custom_call_target="tpu_custom_call" | custom-call | flops 2000000000 | bytes 25165824 | tf_op jit(solution)/shard_map/steps/pallas_call | solution.py:490
  50.8 0.0 copy-start
  50.8 4.1 %copy.17 = f32[3,32,64,128]{3,2,1,0:T(8,128)} copy(f32[3,32,64,128]{3,2,1,0:T(8,128)} %get-tuple-element.12) | data formatting | bytes 6291456
  54.9 0.3 copy-done
  55.2 0.0 copy-start.1
  55.2 2.7 %copy.18 = f32[6,32,64,128]{3,2,1,0:T(8,128)} copy(f32[6,32,64,128]{3,2,1,0:T(8,128)S(1)} %copy-done) | data formatting | bytes 12582912
  57.9 0.0 copy-done.1
  57.9 0.6 copy.19
Async XLA Ops:
  50.8 4.4 %copy-start = (f32[6,32,64,128]{3,2,1,0:T(8,128)S(1)}, f32[6,32,64,128]{3,2,1,0:T(8,128)}, u32[]{:S(2)}) copy-start(f32[6,32,64,128]{3,2,1,0:T(8,128)} %get-tuple-element.13) | copy-start | bytes 18874372
  55.2 2.7 %copy-start.1 = (f32[1,256]{1,0:T(1,128)S(1)}, f32[1,256]{1,0:T(1,128)}, u32[]{:S(2)}) copy-start(f32[1,256]{1,0:T(1,128)} %get-tuple-element.8) | copy-start | bytes 3076

commit v3 on v2

--- a/solution.py
+++ b/solution.py
@@ -89,7 +89,7 @@
     v_out, s_out, strain_out,
     s0, s1, v0, v1, v2, mat, zs, picks, force, asked, inc, inc_scalar, reply, back, flat, along_ref, follow,
     weights, src_x, src_y, src_amp, block, cells, azimuth, gauge,
-    load_sem, send_sem, recv_sem, y_send, y_recv, out_sem, ask_send, ask_recv, reply_send, reply_recv, along_sem,
+    load_sem, send_sem, recv_sem, y_send, y_recv, ask_send, ask_recv, reply_send, reply_recv, along_sem,
 ):
     nx, ny, depth = sizes
     gx, gy = lax.axis_index("gx"), lax.axis_index("gy")
@@ -249,8 +249,8 @@
         def put(f, value):
             updated = old(f) + db * value
             new[f, x + W, PAD + r0 : PAD + r0 + nr, :] = updated
-            if step == 1 and f < 2:
-                v0[f, x, r0 : r0 + nr, :] = updated
+            if step == 1:
+                v_out[f, x, r0 : r0 + nr, :] = updated
 
         put(0, diff_x(s, 0, x, r0, nr, True) + diff_y(s, 2, x, r0, nr, False) + z(0))
         put(1, diff_x(s, 2, x, r0, nr, False) + diff_y(s, 4, x, r0, nr, True) + z(1))
@@ -260,10 +260,11 @@
         put(2, rate + jnp.where(lane == 0, load, 0.0))
 
     def stress_plane(v, s, new, x, r0, nr):
+        px, py = (W, PAD) if new is s1 else (0, 0)
         lam, mu = mat[0, x, r0 : r0 + nr, :], mat[1, x, r0 : r0 + nr, :]
         z = lambda k: zs[k, x, r0 : r0 + nr, :]
         for f, change in enumerate(stress_parts(v, z, x, r0, nr, lam, mu)):
-            new[f, x + W, PAD + r0 : PAD + r0 + nr, :] = own(s, f, x, r0, nr) + change
+            new[f, x + px, py + r0 : py + r0 + nr, :] = own(s, f, x, r0, nr) + change
 
     def interior(update):
         @pl.loop(W, nx - W)
@@ -285,10 +286,10 @@
         functools.partial(velocity_plane, 0, s0),
         functools.partial(stress_plane, v1, s0, s1),
         functools.partial(velocity_plane, 1, s1),
-        functools.partial(stress_plane, v2, s1, s0),
-    )
-
-    def all_edges(phase, done=lambda pieces: None):
+        functools.partial(stress_plane, v2, s1, s_out),
+    )
+
+    def all_edges(phase):
         update = updates[phase]
 
         def piece_of(piece):
@@ -303,10 +304,8 @@
         edges_x(update)
         if phase < 3:
             send(phase + 1, (0, 1))
-        done((0, PARTS - 1))
         for piece in range(1, PARTS - 1):
             piece_of(piece)
-            done((piece,))
 
     v_jobs = ((1, False), (3, False), (5, True))
     s_jobs = ((2, False), (0, True), (1, True))
@@ -360,9 +359,6 @@
             loads[2].wait()
         interior(updates[phase])
         all_edges(phase)
-    v_copy = pltpu.make_async_copy(v2.at[:, planes, rows, :], v_out, out_sem.at[PARTS])
-    v_copy.start()
-
     total = devices * cap
     shift_x, shift_y = (ny * depth).bit_length() - 1, depth.bit_length() - 1
     lane = lax.broadcasted_iota(jnp.int32, (1, depth), 1)
@@ -385,7 +381,7 @@
             y = lax.shift_right_logical(safe, shift_y) & (ny - 1)
             z = jnp.where(cell >= 0, safe & (depth - 1), -1)
             for f in range(2):
-                row = v0[f, x, pl.ds(y, 1), :]
+                row = v_out[f, x, pl.ds(y, 1), :]
                 picks[f, pl.ds(r, 1), :] = jnp.where(lane == z, row, 0.0)
 
     ones = jnp.ones((depth, depth), jnp.float32)
@@ -433,19 +429,7 @@
     def _():
         follow[...] = jnp.zeros(follow.shape, f32)
 
-    s_copies = [
-        pltpu.make_async_copy(
-            s0.at[:, W + piece * part : W + (piece + 1) * part, rows, :],
-            s_out.at[:, piece * part : (piece + 1) * part], out_sem.at[piece],
-        )
-        for piece in range(PARTS)
-    ]
-
-    def write(pieces):
-        for piece in pieces:
-            s_copies[piece].start()
-
-    all_edges(3, write)
+    all_edges(3)
 
     @pl.when(me < devices - 1)
     def _():
@@ -468,10 +452,6 @@
     @pl.when(me > 0)
     def _():
         pass_on.wait_send()
-
-    v_copy.wait()
-    for copy in s_copies:
-        copy.wait()
 
 
 def body(
@@ -490,12 +470,12 @@
     velocity_out, stress_out, strain = pl.pallas_call(
         functools.partial(main_kernel, (nx, ny, depth), cap),
         out_shape=(
-            jax.ShapeDtypeStruct((3, nx, ny, depth), f32),
-            jax.ShapeDtypeStruct((6, nx, ny, depth), f32),
+            pltpu.VMEM((3, nx, ny, depth), f32),
+            pltpu.VMEM((6, nx, ny, depth), f32),
             jax.ShapeDtypeStruct((1, per_device), f32),
         ),
         in_specs=[any_space] * 11,
-        out_specs=(any_space, any_space, vmem),
+        out_specs=(vmem, vmem, vmem),
         scratch_shapes=[
             pltpu.VMEM((6,) + ext, f32),
             pltpu.VMEM((6,) + ext, f32),
@@ -527,7 +507,6 @@
             pltpu.SemaphoreType.DMA((4, 2)),
             pltpu.SemaphoreType.DMA((4, 2, PARTS, 3)),
             pltpu.SemaphoreType.DMA((4, 2, PARTS, 3)),
-            pltpu.SemaphoreType.DMA((PARTS + 1,)),
             pltpu.SemaphoreType.DMA((devices,)),
             pltpu.SemaphoreType.DMA((devices,)),
             pltpu.SemaphoreType.DMA((devices,)),
@@ -535,7 +514,7 @@
             pltpu.SemaphoreType.DMA((2,)),
         ],
         compiler_params=pltpu.CompilerParams(
-            collective_id=0, has_side_effects=True, vmem_limit_bytes=60 * 2**20
+            collective_id=0, has_side_effects=True, vmem_limit_bytes=54 * 2**20
         ),
         cost_estimate=pl.CostEstimate(flops=2 * 10**9, bytes_accessed=24 * 2**20, transcendentals=0),
         name="steps",

time: 58.7 us -> 54.4 us (0.927)
  local copies, waits for them, and re-layouts: 7.68 us -> 4.94 us
  Pallas kernels: 50.2 us -> 48.6 us
    unnamed x7 -> x5, local copies, waits for them, and re-layouts: 7.68 us -> 4.94 us
    pallas_call x1, Pallas kernels: 50.2 us -> 48.6 us  [body(): pl.pallas_call(functools.partial(main_kernel, (nx, ny, depth), cap), out_...]
where the time goes in v3:
time: 54.4 us; the launch traced here: 54.2 us
  Pallas kernels  48.6 us (89%)
  local copies, waits for them, and re-layouts  4.94 us (9%)
  between operations  0.64 us (1%)
    pallas_call x1, Pallas kernels, body(): pl.pallas_call(functools.partial(main_kernel, (nx, ny, depth), cap), out_...  48.6 us
    unnamed x5, local copies, waits for them, and re-layouts  4.94 us

profile of v3, /device:TPU:1, one launch (start us, length us, event | category | flops | bytes accessed | tf_op | source)
XLA Modules:
  0.0 54.2 jit_solution(14722252730341087181)
XLA Ops:
  0.6 48.6 %steps.1 = (f32[3,32,64,128]{3,2,1,0:T(8,128)S(1)}, f32[6,32,64,128]{3,2,1,0:T(8,128)S(1)}, f32[1,256]{1,0:T(1,128)}) custom-call(f32[6,32,64,128]{3,2,1,0:T(8,128)} %stress.1, f32[3,32,64,128]{3,2,1,0:T(8,128)} %velocity.1, f32[3,32,64,128]{3,2,1,0:T(8,128)} %material.1, bf16[2,256,256]{2,1,0:T(8,128)(2,1)} %constant.2.clone.weights_in, s32[2,64]{1,0:T(2,128)} %src_x_in.1, ...), custom_call_target="tpu_custom_call" | custom-call | flops 2000000000 | bytes 25165824 | tf_op jit(solution)/shard_map/steps/pallas_call | solution.py:470
  49.2 1.7 %copy.17 = f32[3,32,64,128]{3,2,1,0:T(8,128)} copy(f32[3,32,64,128]{3,2,1,0:T(8,128)S(1)} %get-tuple-element.9) | data formatting | bytes 6291456
  50.9 0.0 copy-start
  50.9 2.7 %copy.18 = f32[6,32,64,128]{3,2,1,0:T(8,128)} copy(f32[6,32,64,128]{3,2,1,0:T(8,128)S(1)} %get-tuple-element.10) | data formatting | bytes 12582912
  53.6 0.0 copy-done
  53.6 0.6 %copy.19 = f32[256]{0:T(256)} copy(f32[256]{0:T(256)S(1)} %bitcast.5) | data formatting | bytes 2048
Async XLA Ops:
  50.9 2.7 %copy-start = (f32[1,256]{1,0:T(1,128)S(1)}, f32[1,256]{1,0:T(1,128)}, u32[]{:S(2)}) copy-start(f32[1,256]{1,0:T(1,128)} %get-tuple-element.8) | copy-start | bytes 3076
